TPU v7x, 32 devices: a whole 2x2x4 slice. The times are simulated.
32 devices in a mesh: dp: 8 (over z, y), tensor: 4 (over x, core).
Axes of the slice: x: 2, y: 2, z: 4, core: 2. Of those that a mesh axis runs over, the one named last changes fastest.
Arguments:
- final_input: bfloat16 [4096, 4096], P('dp'), may hold values from -20 to 20
- norm_gain: bfloat16 [4096], replicated, may hold values from 0.5 to 2
- value_weight: bfloat16 [4096, 1024], P(None, 'tensor'), may hold values from -0.09375 to 0.09375
- out_weight: bfloat16 [4096, 4096], P('tensor'), may hold values from -0.1875 to 0.1875
- cluster: int32 [4096, 1], P('dp'), may hold values from 0 to 31; in each aligned block of 512 rows (0 to 511, 512 to 1023, ...) at most 32 rows name the same one
- priority: int32 [4096], P('dp'), may hold values from 0 to 4095, each once
Outputs:
- best_match: float32 [4096], P('dp')
Inputs may be any that keep to these rules, and one draw needn't show every extreme that they name: Among the rows of one device (aligned blocks of 512 documents), no cluster holds more than 32 documents, and some cluster holds exactly 32. `priority`: every rank appears exactly once.
All inputs are finite; a program needn't handle non-finite values.
Results may differ from a plain program's by a relative error of at most 0.0012.
Values may be sent and summed in bfloat16 or wider, within the bound.
A program may use at most 128 MiB of HBM per device.

v0:
```python
import jax
import jax.numpy as jnp
from jax import lax
from jax.sharding import PartitionSpec as P

HEADS = 32
KV_HEADS = 8
HEAD_DIM = 128
CLU_DEV = 4


def tile_products(members):
    number_items = members.shape[1]
    slot_count = members.shape[0] * members.shape[2]
    products = jnp.einsum(
        "acbf,ecdf->cabed",
        members,
        members,
        precision=lax.Precision.HIGHEST,
        preferred_element_type=jnp.float32,
    )
    return products.reshape(number_items, slot_count, slot_count)


def cluster_best(products, ranking, sentinel):
    number_items = ranking.shape[1]
    ordered = jnp.transpose(ranking, (1, 0, 2)).reshape(number_items, -1)
    allowed = (ordered[:, None, :] < ordered[:, :, None]) & (ordered[:, None, :] < sentinel)
    highest = jnp.max(jnp.where(allowed, products, -2.0), axis=2)
    highest = jnp.maximum(highest, -1.0)
    return jnp.transpose(
        highest.reshape(number_items, ranking.shape[0], ranking.shape[2]), (1, 0, 2)
    )


def head_terms(values, out_weight, kv_local, group_size):
    model_width = out_weight.shape[1]
    folded = jnp.sum(
        out_weight.reshape(kv_local, group_size, HEAD_DIM, model_width).astype(jnp.float32), axis=1
    )
    folded = folded.reshape(kv_local * HEAD_DIM, model_width)
    upper_part = folded.astype(jnp.bfloat16)
    lower_part = (folded - upper_part.astype(jnp.float32)).astype(jnp.bfloat16)
    upper_term = jnp.dot(values, upper_part, preferred_element_type=jnp.float32)
    return upper_term + jnp.dot(values, lower_part, preferred_element_type=jnp.float32)


def shards(final_input, norm_gain, value_weight, out_weight, cluster, priority):
    doc_rows = final_input.shape[0]
    model_width = final_input.shape[1]
    splits = lax.axis_size("tensor")
    owners = lax.axis_size("dp")
    feature_part = model_width // splits
    bucket_size = max(2, 2 * doc_rows // (CLU_DEV * owners))
    sentinel = owners * doc_rows
    inputs_f32 = final_input.astype(jnp.float32)
    scaling = lax.rsqrt(jnp.mean(inputs_f32 * inputs_f32, axis=1, keepdims=True) + 1e-05)
    normed = (inputs_f32 * scaling * norm_gain.astype(jnp.float32)).astype(jnp.bfloat16)
    values = jnp.dot(normed, value_weight, preferred_element_type=jnp.float32).astype(jnp.bfloat16)
    kv_local = value_weight.shape[1] // HEAD_DIM
    group_size = HEADS // KV_HEADS
    partial_out = (
        head_terms(values, out_weight, kv_local, group_size)
        .astype(jnp.bfloat16)
        .astype(jnp.float32)
    )
    feature_start = lax.axis_index("tensor") * feature_part
    summed = lax.psum(partial_out.astype(jnp.bfloat16), "tensor").astype(jnp.float32)
    hidden_full = inputs_f32 + summed
    squares = jnp.sum(hidden_full * hidden_full, axis=1)
    hidden = lax.dynamic_slice_in_dim(hidden_full, feature_start, feature_part, 1)
    embedded = hidden * lax.rsqrt(squares + 1e-06)[:, None]
    cluster_ids = cluster[:, 0]
    positions = jnp.arange(doc_rows, dtype=jnp.int32)
    earlier = (cluster_ids[:, None] == cluster_ids[None, :]) & (
        positions[None, :] < positions[:, None]
    )
    slot_index = jnp.sum(earlier.astype(jnp.int32), axis=1)
    flat_slot = cluster_ids * bucket_size + slot_index
    slot_total = owners * CLU_DEV * bucket_size
    send_rows = jnp.zeros((slot_total, feature_part), jnp.float32).at[flat_slot].set(embedded)
    send_rows = send_rows.reshape(owners, CLU_DEV, bucket_size, feature_part)
    send_ranks = jnp.full((slot_total,), sentinel, jnp.int32).at[flat_slot].set(priority)
    send_ranks = send_ranks.reshape(owners, CLU_DEV, bucket_size)
    members = lax.all_to_all(send_rows, "dp", split_axis=0, concat_axis=0, tiled=True)
    ranking = lax.all_to_all(send_ranks, "dp", split_axis=0, concat_axis=0, tiled=True)
    products = lax.psum(tile_products(members), "tensor")
    highest = cluster_best(products, ranking, sentinel)
    returned = lax.all_to_all(highest, "dp", split_axis=0, concat_axis=0, tiled=True)
    return returned.reshape(-1)[flat_slot]


def solution(mesh):
    in_specs = (P("dp", None), P(), P(None, "tensor"), P("tensor", None), P("dp", None), P("dp"))
    out_specs = P("dp")
    return jax.shard_map(shards, mesh=mesh, in_specs=in_specs, out_specs=out_specs, check_vma=False)
```

profile of v0, /device:TPU:0, one launch (start us, length us, event | category | flops | bytes accessed | tf_op | source)
XLA Modules:
  0.0 305.9 jit_solution(6012590431231733487)
XLA Ops:
  6.5 5.5 %convert_reduce_fusion = f32[2,128,4096]{2,1,0:T(8,128)S(1)} fusion(bf16[2,4,128,4096]{3,2,1,0:T(8,128)(2,1)} %bitcast.29), kind=kLoop, calls=%fused_computation.3 | loop fusion | flops 7340032 | bytes 12582912 | tf_op jit(solution)/shard_map/reduce_sum | solution.py:38
  12.1 0.6 fusion.8
  12.7 0.1 copy-done.4
  12.8 1.5 copy-done.2
  14.3 0.9 fusion
  15.2 1.3 fusion.15
  16.5 1.3 fusion.22
  17.8 3.2 %add_convert_fusion = bf16[512,4096]{1,0:T(8,128)(2,1)} fusion(f32[512,4096]{1,0:T(8,128)S(1)} %fusion.22, bf16[512,256]{1,0:T(8,128)(2,1)S(1)} %fusion.15, bf16[256,4096]{1,0:T(8,128)(2,1)S(1)} %get-tuple-element.5), kind=kOutput, calls=%fused_computation.11 | convolution fusion | flops 1077936128 | bytes 14942208 | tf_op jit(solution)/shard_map/dot_general | solution.py:45
  21.1 0.6 copy-done.3
  21.7 0.2 convert_reduce_fusion.1
  21.9 87.4 %all-reduce.3.cloned.1.call-done = bf16[512,4096]{1,0:T(8,128)(2,1)} async-done(((bf16[512,4096]{1,0:T(8,128)(2,1)}), bf16[512,4096]{1,0:T(8,128)(2,1)}) %all-reduce.3.cloned.1.call-update) | async-done | bytes 4194320 | tf_op jit(solution)/shard_map/psum | solution.py:68
  109.3 8.0 %multiply_reduce_fusion = (f32[512]{0:T(512)S(1)}, f32[512,4096]{1,0:T(8,128)}) fusion(bf16[512,4096]{1,0:T(8,128)(2,1)} %all-reduce.3.cloned.1.call-done, bf16[512,4096]{1,0:T(8,128)(2,1)} %param.6), kind=kLoop, calls=%fused_computation.10 | loop fusion | flops 10485248 | bytes 16779264 | tf_op jit(solution)/shard_map/reduce_sum | solution.py:70
  117.4 5.7 %scatter_custom_fusion.1 = f32[1024,1024]{1,0:T(8,128)} fusion(s32[512]{0:T(512)S(1)} %bitcast.33, f32[512,4096]{1,0:T(8,128)} %get-tuple-element.8, s32[]{:T(128)} %constant.14.clone.1, s32[]{:T(128)S(6)} %select_n.14, f32[]{:T(128)} %constant.16.clone.1, f32[512]{0:T(512)S(1)} %add_rsqrt_fusion), kind=kCustom, calls=%fused_computation.21 | custom fusion | flops 524288 | bytes 6294532 | tf_op jit(solution)/shard_map/scatter | solution.py:81
  123.1 98.8 %all_to_all.15 = f32[8,4,32,1024]{3,2,1,0:T(8,128)S(1)} all-to-all(f32[8,4,32,1024]{3,2,1,0:T(8,128)} %bitcast.28), channel_id=1, replica_groups=mesh['dp'=8,'tensor'=4] {'dp'}, dimensions={0} | all-to-all | bytes 8388608 | tf_op jit(solution)/shard_map/all_to_all | solution.py:85
  221.8 13.6 %fusion.5 = f32[4,8,32,8,32]{4,2,3,1,0:T(8,128)S(1)} fusion(f32[8,4,32,1024]{3,2,1,0:T(8,128)S(1)} %all_to_all.15), kind=kOutput, calls=%fused_computation.13 | convolution fusion | flops 3221225472 | bytes 5242880 | tf_op jit(solution)/shard_map/acbf,ecdf->cabed/dot_general | solution.py:15
  235.4 5.8 %copy.21 = f32[4,8,32,8,32]{4,3,2,1,0:T(8,128)} copy(f32[4,8,32,8,32]{4,2,3,1,0:T(8,128)S(1)} %fusion.5) | data formatting | bytes 2097152 | tf_op jit(solution)/shard_map/acbf,ecdf->cabed/dot_general | solution.py:15
  241.2 4.2 %reshape.49 = f32[4,256,256]{2,1,0:T(8,128)} reshape(f32[4,8,32,8,32]{4,3,2,1,0:T(8,128)} %copy.21) | data formatting | bytes 2097152 | tf_op jit(solution)/shard_map/reshape | solution.py:22
  245.4 2.6 scatter_custom_fusion
  248.1 0.1 reshape.82
  248.2 9.6 %all_to_all.16 = s32[8,1,128]{2,1,0:T(1,128)S(1)} all-to-all(s32[8,1,128]{2,1,0:T(1,128)S(1)} %reshape.82), channel_id=1, replica_groups=mesh['dp'=8,'tensor'=4] {'dp'}, dimensions={0} | all-to-all | bytes 8192 | tf_op jit(solution)/shard_map/all_to_all | solution.py:86
  257.8 0.5 broadcast.41
  258.3 0.7 reduce
  259.1 0.1 lt.52
  259.2 20.8 %all-reduce.5.cloned.1.call-done = f32[4,256,256]{2,1,0:T(8,128)} async-done(((f32[4,256,256]{2,1,0:T(8,128)}), f32[4,256,256]{2,1,0:T(8,128)}) %all-reduce.5.cloned.1.call-update) | async-done | bytes 1048592 | tf_op jit(solution)/shard_map/psum | solution.py:87
  279.9 1.6 select_reduce_fusion
  281.6 0.7 reshape.84
  282.3 5.5 %all-to-all-start.2 = ((f32[8,1,128]{2,1,0:T(1,128)}), f32[8,1,128]{2,1,0:T(1,128)S(1)}, u32[]{:S(2)}, u32[]{:S(2)}) async-start(f32[8,1,128]{2,1,0:T(1,128)} %reshape.84), calls=%async_computation.2 | async-start | bytes 8192 | tf_op jit(solution)/shard_map/all_to_all | solution.py:89
  287.9 6.5 %all-to-all-done.2 = f32[8,1,128]{2,1,0:T(1,128)S(1)} async-done(((f32[8,1,128]{2,1,0:T(1,128)}), f32[8,1,128]{2,1,0:T(1,128)S(1)}, u32[]{:S(2)}, u32[]{:S(2)}) %all-to-all-start.2) | async-done | bytes 4128 | tf_op jit(solution)/shard_map/all_to_all | solution.py:89
  294.3 0.5 broadcast.42
  294.8 0.7 reduce.1
  295.6 0.1 reshape.50
  295.6 3.4 %gather_fusion = f32[512]{0:T(512)} fusion(f32[1024]{0:T(1024)S(1)} %reshape.50, s32[1024]{0:T(1024)S(1)} %pad_clamp_fusion), kind=kCustom, calls=%fused_computation | custom fusion | bytes 6144 | tf_op jit(solution)/shard_map/gather | solution.py:90
  (24 shorter events, 0.5 us)
Async XLA Ops:
  6.5 8.6 %copy-start = (bf16[4096,256]{1,0:T(8,128)(2,1)S(1)}, bf16[4096,256]{1,0:T(8,128)(2,1)}, u32[]{:S(2)}) copy-start(bf16[4096,256]{1,0:T(8,128)(2,1)} %param.8) | copy-start | bytes 6291460
  6.5 102.8 %all-reduce.3.cloned.1.call-start = ((), (), s32[]{:S(2)}) async-start(), calls=%async_computation.3 | async-start | bytes 8388608 | tf_op jit(solution)/shard_map/psum | solution.py:68
  12.1 0.7 copy-start.4
  12.1 2.2 copy-start.2
  21.0 0.7 copy-start.3
  21.0 258.9 %all-reduce.5.cloned.1.call-start = ((), (), s32[]{:S(2)}) async-start(), calls=%async_computation.4 | async-start | bytes 2097152 | tf_op jit(solution)/shard_map/psum | solution.py:87
  235.4 63.6 %copy-start.1 = (bf16[4096,256]{1,0:T(8,128)(2,1)S(1)}, bf16[4096,256]{1,0:T(8,128)(2,1)}, u32[]{:S(2)}) copy-start(bf16[4096,256]{1,0:T(8,128)(2,1)} %param.8) | copy-start | bytes 6291460
  282.3 12.0 %all-to-all-start.2 = ((f32[8,1,128]{2,1,0:T(1,128)}), f32[8,1,128]{2,1,0:T(1,128)S(1)}, u32[]{:S(2)}, u32[]{:S(2)}) async-start(f32[8,1,128]{2,1,0:T(1,128)} %reshape.84), calls=%async_computation.2 | async-start | bytes 8192 | tf_op jit(solution)/shard_map/all_to_all | solution.py:89
Sparse Core Ops, SparseCore 0:
  21.1 88.1 all-reduce.2
  245.5 34.3 all-reduce.4
where the time goes:
time: 306 us
  waiting for transfers between devices  115 us (38%)
  blocking collectives  108 us (35%)
  other arithmetic  23.9 us (8%)
  local copies, waits for them, and re-layouts  20.5 us (7%)
  matrix products  19.4 us (6%)
  between operations  13.5 us (4%)
  starting transfers between devices  5.56 us (2%)
    all_to_all x1, blocking collectives, shards(): lax.all_to_all(send_rows, 'dp', split_axis=0, concat_axis=0, tiled=True)  98.8 us
    psum x1, waiting for transfers between devices, shards(): lax.psum(partial_out.astype(jnp.bfloat16), 'tensor').astype(jnp.float32)  87.4 us
    psum x1, waiting for transfers between devices, shards(): products = lax.psum(tile_products(members), 'tensor')  20.8 us
    dot_general x1, matrix products, tile_products(): jnp.einsum('acbf,ecdf->cabed', members, members, precision=lax.Precision....  13.6 us
    all_to_all x1, blocking collectives, shards(): lax.all_to_all(send_ranks, 'dp', split_axis=0, concat_axis=0, tiled=True)  9.62 us
    reduce_sum x1, other arithmetic, shards(): squares = jnp.sum(hidden_full * hidden_full, axis=1)  8.03 us
    all_to_all x1, waiting for transfers between devices, shards(): lax.all_to_all(highest, 'dp', split_axis=0, concat_axis=0, tiled=True)  6.46 us
  transfers between devices with their start and end apart: 3, of which 3 were waited for; matrix products, arithmetic and copies ran while one was open for 1% of the time, Pallas kernels for 0%

commit v1 on v0

v1 whole, which is shorter than its diff:
```python
import functools

import jax
import jax.numpy as jnp
from jax import lax
from jax.experimental import pallas as pl
from jax.experimental.pallas import tpu as pltpu
from jax.sharding import PartitionSpec as P

HEADS = 32
KV_HEADS = 8
HEAD_DIM = 128
CLU_DEV = 4
CHUNKS = 4
MESH = pl.DeviceIdType.MESH
BF16 = jnp.bfloat16
F32 = jnp.float32
I32 = jnp.int32


def iota(shape, dim):
    return lax.broadcasted_iota(I32, shape, dim)


def kernel(
    owners, bucket,
    x_hbm, gain_ref, vw_hbm, ow_hbm, cluster_ref, priority_ref, out_ref,
    x_v, vw_v, ow_v, values, send_a, keep_a, recv_a, send_b, recv_b,
    place, send_c, recv_c, send_r, recv_r, gram, recv_e, send_f, recv_f, best_t, send_h, recv_h,
    in_sem, a_s, a_r, b_s, b_r, c_s, c_r, r_s, r_r, e_s, e_r, f_s, f_r, g_s, g_r, h_s, h_r,
):
    rows, width = x_v.shape
    chunk = recv_b.shape[2]
    chunks = recv_b.shape[0]
    part = chunk * chunks
    per_owner = CLU_DEV * bucket
    capacity = owners * bucket
    sentinel = owners * rows
    me = lax.axis_index("dp")
    t = lax.axis_index("tensor")
    xh, core = t // 2, t % 2
    partner = 2 * xh + (1 - core)
    across = 2 * (1 - xh) + core
    half = rows // 2

    def load_x(i):
        span = pl.ds(i * half, half)
        return pltpu.make_async_copy(x_hbm.at[span], x_v.at[span], in_sem.at[i])

    load_vw = pltpu.make_async_copy(vw_hbm, vw_v, in_sem.at[2])
    load_ow = pltpu.make_async_copy(ow_hbm, ow_v, in_sem.at[3])
    load_x(0).start()
    load_vw.start()
    load_x(1).start()
    load_ow.start()

    barrier = pltpu.get_barrier_semaphore()

    def greet(o, _):
        pl.semaphore_signal(barrier, inc=1, device_id=(lax.rem(me + o, owners), t), device_id_type=MESH)
        return 0

    for o in range(1, 4):
        pl.semaphore_signal(barrier, inc=1, device_id=(me, lax.rem(t + o, 4)), device_id_type=MESH)
    lax.fori_loop(1, owners, greet, 0)

    def project(i, _):
        span = pl.ds(pl.multiple_of(i * half, half), half)
        xs = x_v[span, :].astype(F32)
        scaling = lax.rsqrt(jnp.sum(xs * xs, axis=1, keepdims=True) * (1.0 / width) + 1e-05)
        normed = (xs * scaling * gain_ref[...].astype(F32)).astype(BF16)
        values[span, :] = jnp.dot(normed, vw_v[...], preferred_element_type=F32).astype(BF16)
        return 0

    load_x(0).wait()
    load_x(1).wait()
    load_vw.wait()
    lax.fori_loop(0, 2, project, 0)
    load_ow.wait()

    def copy_a(k):
        return pltpu.make_async_remote_copy(
            send_a.at[k], recv_a.at[k], a_s.at[k], a_r.at[k], device_id=(me, partner), device_id_type=MESH)

    def copy_b(k):
        return pltpu.make_async_remote_copy(
            send_b.at[k], recv_b.at[k], b_s.at[k], b_r.at[k], device_id=(me, across), device_id_type=MESH)

    def copy_c(k, to, frm):
        return pltpu.make_async_remote_copy(
            send_c.at[k, to], recv_c.at[k, frm], c_s.at[k, to], c_r.at[k, frm],
            device_id=(to, t), device_id_type=MESH)

    def copy_r(to, frm):
        return pltpu.make_async_remote_copy(
            send_r.at[to], recv_r.at[frm], r_s.at[to], r_r.at[frm], device_id=(to, t), device_id_type=MESH)

    def copy_h(to, frm):
        return pltpu.make_async_remote_copy(
            send_h, recv_h.at[frm], h_s.at[to], h_r.at[frm], device_id=(to, t), device_id_type=MESH)

    def term(quarter, k):
        columns = pl.ds(pl.multiple_of(quarter * part + k * chunk, chunk), chunk)
        w = ow_v[:, columns].astype(F32)
        kv_local = values.shape[1] // HEAD_DIM
        w = w.reshape(kv_local, HEADS // KV_HEADS, HEAD_DIM, chunk)
        w = jnp.sum(w, axis=1).reshape(kv_local * HEAD_DIM, chunk).astype(BF16)
        return jnp.dot(values[...], w, preferred_element_type=F32).astype(BF16)

    def stage_a(k, _):
        for h in range(2):
            send_a[k, h] = term(2 * h + 1 - core, k)

        @pl.when(k == 0)
        def _():
            pl.semaphore_wait(barrier, 3 + owners - 1)

        copy_a(k).start()
        for h in range(2):
            keep_a[k, h] = term(2 * h + core, k)

        @pl.when(k > 0)
        def _():
            stage_b(k - 1)

        return 0

    def stage_b(k):
        copy_a(k).wait_recv()
        send_b[k] = (keep_a[k, 1 - xh].astype(F32) + recv_a[k, 1 - xh].astype(F32)).astype(BF16)
        copy_b(k).start()

    lax.fori_loop(0, chunks, stage_a, 0)
    stage_b(chunks - 1)

    cluster_col = cluster_ref[...]
    square = (rows, rows)
    i0, i1 = iota(square, 0), iota(square, 1)
    cluster_row = jnp.sum(jnp.where(i0 == i1, cluster_col, 0), axis=0, keepdims=True)
    slot_row = jnp.sum(
        jnp.where((cluster_col == cluster_row) & (i0 < i1), 1, 0), axis=0, keepdims=True)
    flat_row = cluster_row * bucket + slot_row
    place[...] = jnp.where(iota(place.shape, 0) == flat_row, 1.0, 0.0).astype(BF16)

    rank = priority_ref[...]
    high, low = (rank // 128).astype(F32), (rank % 128).astype(F32)
    line = iota((8, rows), 0)
    meta = jnp.where(line == 0, high, jnp.where(line == 1, low, jnp.where(line == 2, 1.0, 0.0)))
    meta = meta.astype(BF16)

    def rank_block(to, _):
        s = iota((128, rows), 0)
        hit = (s + to * per_owner == flat_row) & (s < per_owner)
        got = lax.dot_general(
            meta, jnp.where(hit, 1.0, 0.0).astype(BF16), (((1,), (1,)), ((), ())),
            preferred_element_type=F32)
        line = got[0:1] * 128.0 + got[1:2] + (1.0 - got[2:3]) * float(sentinel)
        send_r[to] = jnp.broadcast_to(line, (8, 128))
        return 0

    lax.fori_loop(0, owners, rank_block, 0)
    recv_r[me] = send_r[me]

    def start_r(o, _):
        copy_r(lax.rem(me + o, owners), me).start()
        return 0

    lax.fori_loop(1, owners, start_r, 0)

    def stage_c(k, _):
        copy_b(k).wait_recv()
        columns = pl.ds(pl.multiple_of(t * part + k * chunk, chunk), chunk)
        attention = keep_a[k, xh].astype(F32) + recv_a[k, xh].astype(F32) + recv_b[k].astype(F32)
        hidden = (x_v[:, columns].astype(F32) + attention).astype(BF16)
        placed = jnp.dot(place[...], hidden, preferred_element_type=F32).astype(BF16)
        send_c[k] = placed.reshape(owners, per_owner, chunk)

        def start_c(o, _):
            copy_c(k, lax.rem(me + o, owners), me).start()
            return 0

        lax.fori_loop(1, owners, start_c, 0)
        recv_c[k, me] = send_c[k, me]
        return 0

    lax.fori_loop(0, chunks, stage_c, 0)

    gram[...] = jnp.zeros_like(gram)

    def stage_d(k, _):
        def wait_c(o, _):
            copy_c(k, me, lax.rem(me + o, owners)).wait_recv()
            return 0

        lax.fori_loop(1, owners, wait_c, 0)
        for c in range(CLU_DEV):
            if bucket % 16 == 0:
                members = recv_c[k, :, c * bucket:(c + 1) * bucket, :].reshape(capacity, chunk)
            else:
                every = recv_c[k].reshape(owners * per_owner, chunk)
                shape = (capacity, owners * per_owner)
                r = iota(shape, 0)
                pick = (r // bucket) * per_owner + c * bucket + r % bucket == iota(shape, 1)
                members = jnp.dot(
                    jnp.where(pick, 1.0, 0.0).astype(BF16), every, preferred_element_type=F32).astype(BF16)
            gram[c] += lax.dot_general(
                members, members, (((1,), (1,)), ((), ())), preferred_element_type=F32)
        return 0

    lax.fori_loop(0, chunks, stage_d, 0)

    def copy_e(h):
        return pltpu.make_async_remote_copy(
            gram.at[2 * h + 1 - core], recv_e.at[h], e_s.at[h], e_r.at[h],
            device_id=(me, partner), device_id_type=MESH)

    copy_f = pltpu.make_async_remote_copy(
        send_f, recv_f, f_s, f_r, device_id=(me, across), device_id_type=MESH)
    copy_e(1 - xh).start()
    copy_e(xh).start()

    def wait_r(o, _):
        copy_r(me, lax.rem(me + o, owners)).wait_recv()
        return 0

    lax.fori_loop(1, owners, wait_r, 0)
    ranks = recv_r[:, 0, :]
    r = iota((capacity, owners), 0)
    expand = jnp.where(r // bucket == iota((capacity, owners), 1), 1.0, 0.0)
    spread = jnp.dot(expand, ranks, precision=lax.Precision.HIGHEST, preferred_element_type=F32)
    r = iota((capacity, 128), 0)
    rank_col = jnp.sum(
        jnp.where(iota((capacity, 128), 1) == t * bucket + r % bucket, spread, 0.0), axis=1, keepdims=True)
    eye = iota((capacity, capacity), 0) == iota((capacity, capacity), 1)
    rank_row = jnp.sum(jnp.where(eye, rank_col, 0.0), axis=0, keepdims=True)

    copy_e(1 - xh).wait_recv()
    send_f[...] = gram[2 * (1 - xh) + core] + recv_e[1 - xh]
    copy_f.start()
    copy_e(xh).wait_recv()
    mine = gram[2 * xh + core] + recv_e[xh]
    copy_f.wait_recv()
    total = mine + recv_f[...]
    diagonal = jnp.where(eye, total, 0.0)
    norm_row = lax.rsqrt(jnp.sum(diagonal, axis=0, keepdims=True) + 1e-06)
    norm_col = lax.rsqrt(jnp.sum(diagonal, axis=1, keepdims=True) + 1e-06)
    similarity = total * norm_col * norm_row
    highest = jnp.max(jnp.where(rank_col < rank_row, similarity, -2.0), axis=0, keepdims=True)
    highest = jnp.maximum(highest, -1.0)
    best_t[t] = jnp.broadcast_to(highest, (8, capacity))

    def copy_g(to, frm):
        return pltpu.make_async_remote_copy(
            best_t.at[frm], best_t.at[frm], g_s.at[to], g_r.at[frm], device_id=(me, to), device_id_type=MESH)

    for o in range(1, 4):
        copy_g(lax.rem(t + o, 4), t).start()
    for o in range(1, 4):
        copy_g(t, lax.rem(t + o, 4)).wait_recv()
    line = iota((8, capacity), 0)
    rows_h = jnp.zeros((8, capacity), F32)
    for c in range(CLU_DEV):
        rows_h = jnp.where(line == c, best_t[c], rows_h)
    send_h[...] = rows_h

    def start_h(o, _):
        copy_h(lax.rem(me + o, owners), me).start()
        return 0

    lax.fori_loop(1, owners, start_h, 0)
    recv_h[me] = rows_h

    def wait_h(o, _):
        copy_h(me, lax.rem(me + o, owners)).wait_recv()
        return 0

    pick = jnp.where(iota((capacity, rows), 0) == me * bucket + slot_row, 1.0, 0.0)
    lax.fori_loop(1, owners, wait_h, 0)
    returned = recv_h[...].reshape(owners * 8, capacity)
    found = jnp.dot(returned, pick, precision=lax.Precision.HIGHEST, preferred_element_type=F32)
    where = (cluster_row // CLU_DEV) * 8 + cluster_row % CLU_DEV
    out_ref[...] = jnp.sum(
        jnp.where(iota((owners * 8, rows), 0) == where, found, 0.0), axis=0, keepdims=True)

    def sent_k(k, _):
        copy_a(k).wait_send()
        copy_b(k).wait_send()

        def sent_c(o, _):
            copy_c(k, lax.rem(me + o, owners), me).wait_send()
            return 0

        lax.fori_loop(1, owners, sent_c, 0)
        return 0

    lax.fori_loop(0, chunks, sent_k, 0)

    def sent(o, _):
        to = lax.rem(me + o, owners)
        copy_r(to, me).wait_send()
        copy_h(to, me).wait_send()
        return 0

    lax.fori_loop(1, owners, sent, 0)
    copy_e(1 - xh).wait_send()
    copy_e(xh).wait_send()
    copy_f.wait_send()
    for o in range(1, 4):
        copy_g(lax.rem(t + o, 4), t).wait_send()


def shards(final_input, norm_gain, value_weight, out_weight, cluster, priority):
    rows, width = final_input.shape
    owners = lax.axis_size("dp")
    tensor = lax.axis_size("tensor")
    part = width // tensor
    chunk = part // CHUNKS
    bucket = max(2, 2 * rows // (CLU_DEV * owners))
    per_owner = CLU_DEV * bucket
    capacity = owners * bucket
    kv = value_weight.shape[1]
    vmem = pl.BlockSpec(memory_space=pltpu.VMEM)
    anywhere = pl.BlockSpec(memory_space=pl.ANY)
    dma = pltpu.SemaphoreType.DMA
    best = pl.pallas_call(
        functools.partial(kernel, owners, bucket),
        out_shape=jax.ShapeDtypeStruct((1, rows), F32),
        in_specs=[anywhere, vmem, anywhere, anywhere, vmem, vmem],
        out_specs=vmem,
        scratch_shapes=[
            pltpu.VMEM((rows, width), BF16),
            pltpu.VMEM((width, kv), BF16),
            pltpu.VMEM(out_weight.shape, BF16),
            pltpu.VMEM((rows, kv), BF16),
            pltpu.VMEM((CHUNKS, 2, rows, chunk), BF16),
            pltpu.VMEM((CHUNKS, 2, rows, chunk), BF16),
            pltpu.VMEM((CHUNKS, 2, rows, chunk), BF16),
            pltpu.VMEM((CHUNKS, rows, chunk), BF16),
            pltpu.VMEM((CHUNKS, rows, chunk), BF16),
            pltpu.VMEM((owners * per_owner, rows), BF16),
            pltpu.VMEM((CHUNKS, owners, per_owner, chunk), BF16),
            pltpu.VMEM((CHUNKS, owners, per_owner, chunk), BF16),
            pltpu.VMEM((owners, 8, 128), F32),
            pltpu.VMEM((owners, 8, 128), F32),
            pltpu.VMEM((CLU_DEV, capacity, capacity), F32),
            pltpu.VMEM((2, capacity, capacity), F32),
            pltpu.VMEM((capacity, capacity), F32),
            pltpu.VMEM((capacity, capacity), F32),
            pltpu.VMEM((CLU_DEV, 8, capacity), F32),
            pltpu.VMEM((8, capacity), F32),
            pltpu.VMEM((owners, 8, capacity), F32),
            dma((4,)),
            dma((CHUNKS,)), dma((CHUNKS,)),
            dma((CHUNKS,)), dma((CHUNKS,)),
            dma((CHUNKS, owners)), dma((CHUNKS, owners)),
            dma((owners,)), dma((owners,)),
            dma((2,)), dma((2,)),
            dma, dma,
            dma((4,)), dma((4,)),
            dma((owners,)), dma((owners,)),
        ],
        compiler_params=pltpu.CompilerParams(
            collective_id=0, has_side_effects=True, vmem_limit_bytes=56 * 1024 * 1024),
        cost_estimate=pl.CostEstimate(flops=6_000_000_000, bytes_accessed=16_000_000, transcendentals=0),
    )(final_input, norm_gain.reshape(1, width), value_weight, out_weight, cluster, priority.reshape(1, rows))
    return best.reshape(rows)


def solution(mesh):
    in_specs = (P("dp", None), P(), P(None, "tensor"), P("tensor", None), P("dp", None), P("dp"))
    out_specs = P("dp")
    return jax.shard_map(shards, mesh=mesh, in_specs=in_specs, out_specs=out_specs, check_vma=False)
```

time: 306 us -> 89.6 us (0.29)
  waiting for transfers between devices: 115 us -> 0 us
  blocking collectives: 108 us -> 0 us
  Pallas kernels: 0 us -> 85.2 us
  other arithmetic: 23.9 us -> 0 us
  matrix products: 19.4 us -> 0 us
  local copies, waits for them, and re-layouts: 20.5 us -> 4.08 us
  between operations: 13.5 us -> 0.01 us
  starting transfers between devices: 5.56 us -> 0 us
    all_to_all x2 -> x0, blocking collectives: 108 us -> none  [the longest x1 98.8 us: shards(): lax.all_to_all(send_rows, 'dp', split_axis=0, concat_axis=0, tiled=True)]
    psum x2 -> x0, waiting for transfers between devices: 108 us -> none  [the longest x1 87.4 us: shards(): lax.psum(partial_out.astype(jnp.bfloat16), 'tensor').astype(jnp.float32)]
    pallas_call x0 -> x1, Pallas kernels: none -> 85.2 us  [shards(): pl.pallas_call(functools.partial(kernel, owners, bucket), out_shape=jax.S...]
    dot_general x4 -> x0, matrix products: 19.4 us -> none  [the longest x1 13.6 us: tile_products(): jnp.einsum('acbf,ecdf->cabed', members, members, precision=lax.Precision....]
    reduce_sum x4 -> x0, other arithmetic: 14.7 us -> none  [the longest x1 8.03 us: shards(): squares = jnp.sum(hidden_full * hidden_full, axis=1)]
    all_to_all x1 -> x0, waiting for transfers between devices: 6.46 us -> none  [shards(): lax.all_to_all(highest, 'dp', split_axis=0, concat_axis=0, tiled=True)]
    dot_general x1 -> x0, local copies, waits for them, and re-layouts: 5.75 us -> none  [tile_products(): jnp.einsum('acbf,ecdf->cabed', members, members, precision=lax.Precision....]
    scatter x1 -> x0, other arithmetic: 5.68 us -> none  [shards(): jnp.zeros((slot_total, feature_part), jnp.float32).at[flat_slot]]
  transfers between devices with their start and end apart: 3 -> 0, of which waited for: 3 -> 0; matrix products, arithmetic and copies ran while one was open for 1% -> 0% of each run, Pallas kernels for 0% -> 0%
where the time goes in v1:
time: 89.6 us; the launch traced here: 89.3 us
  Pallas kernels  85.2 us (95%)
  local copies, waits for them, and re-layouts  4.08 us (5%)
    pallas_call x1, Pallas kernels, shards(): pl.pallas_call(functools.partial(kernel, owners, bucket), out_shape=jax.S...  85.2 us
    unnamed x2, local copies, waits for them, and re-layouts  2.77 us

profile of v1, /device:TPU:0, one launch (start us, length us, event | category | flops | bytes accessed | tf_op | source)
XLA Modules:
  0.0 89.3 jit_solution(10917073761890444406)
XLA Ops:
  0.0 1.3 %reshape.9.gain_ref = bf16[1,4096]{1,0:T(2,128)(2,1)} reshape(bf16[4096]{0:T(1024)(128)(2,1)} %param.7) | data formatting | bytes 16384 | tf_op jit(solution)/shard_map/reshape | solution.py:365
  1.3 1.5 %copy.7.cluster_ref = s32[512,1]{1,0:T(8,128)} copy(s32[512,1]{0,1:T(1,128)} %param.10) | data formatting | bytes 4096 | tf_op args[4]
  2.8 85.2 %shard_map.64 = f32[1,512]{1,0:T(1,128)} custom-call(bf16[512,4096]{1,0:T(8,128)(2,1)} %x_hbm.1, bf16[1,4096]{1,0:T(2,128)(2,1)} %reshape.9.gain_ref, bf16[4096,256]{1,0:T(8,128)(2,1)} %vw_hbm.1, bf16[1024,4096]{1,0:T(8,128)(2,1)} %ow_hbm.1, s32[512,1]{1,0:T(8,128)} %copy.7.cluster_ref, s32[1,512]{1,0:T(1,128)} %bitcast.3), custom_call_target="tpu_custom_call" | custom-call | flops 6000000000 | bytes 16000000 | tf_op jit(solution)/shard_map/pallas_call | solution.py:325
  88.1 1.2 %copy.9 = f32[512]{0:T(512)} copy(f32[512]{0:T(512)} %bitcast.2) | data formatting | bytes 4096

commit v2 on v1

v2 whole, which is shorter than its diff:
```python
import functools

import jax
import jax.numpy as jnp
from jax import lax
from jax.experimental import pallas as pl
from jax.experimental.pallas import tpu as pltpu
from jax.sharding import PartitionSpec as P

HEADS = 32
KV_HEADS = 8
HEAD_DIM = 128
CLU_DEV = 4
CHUNKS = 8
LAG = 5
MESH = pl.DeviceIdType.MESH
BF16 = jnp.bfloat16
F32 = jnp.float32
I32 = jnp.int32


def iota(shape, dim):
    return lax.broadcasted_iota(I32, shape, dim)


def drain(ref, sem):
    pltpu.make_async_copy(ref, ref, sem).wait()


def kernel(
    owners, bucket,
    x_hbm, gain_ref, vw_hbm, ow_hbm, cluster_ref, priority_ref, out_ref,
    x_v, vw_v, ow_v, values, send_a, keep_a, recv_a, send_b, recv_b,
    place, send_c, recv_c, send_r, recv_r, gram, recv_e, send_f, recv_f, best_t, send_h, recv_h,
    in_sem, a_s, a_r, b_s, b_r, c_s, c_r, r_s, r_r, e_s, e_r, f_s, f_r, g_s, g_r, h_s, h_r,
):
    rows, width = x_v.shape
    chunks, _, chunk = recv_b.shape
    part = chunk * chunks
    side = recv_c.shape[3]
    per_owner = 2 * side
    capacity = owners * bucket
    sentinel = owners * rows
    me = lax.axis_index("dp")
    t = lax.axis_index("tensor")
    xh, core = t // 2, t % 2
    partner = 2 * xh + (1 - core)
    across = 2 * (1 - xh) + core
    half = rows // 2

    def peer(o):
        found, bit = 0, 1
        while bit < owners:
            found = found + lax.rem(me // bit + o // bit, 2) * bit
            bit = 2 * bit
        return found

    def each_peer(act):
        def step(i, _):
            act(peer(owners - 1 - i))
            return 0

        lax.fori_loop(0, owners - 1, step, 0)

    def load_x(i):
        span = pl.ds(i * half, half)
        return pltpu.make_async_copy(x_hbm.at[span], x_v.at[span], in_sem.at[i])

    load_vw = pltpu.make_async_copy(vw_hbm, vw_v, in_sem.at[2])
    load_ow = pltpu.make_async_copy(ow_hbm, ow_v, in_sem.at[3])
    load_x(0).start()
    load_vw.start()
    load_x(1).start()
    load_ow.start()

    barrier = pltpu.get_barrier_semaphore()
    for o in range(1, 4):
        pl.semaphore_signal(barrier, inc=1, device_id=(me, lax.rem(t + o, 4)), device_id_type=MESH)
    each_peer(lambda to: pl.semaphore_signal(barrier, inc=1, device_id=(to, t), device_id_type=MESH))

    cluster_row = cluster_ref[...]
    square = (rows, rows)
    i0, i1 = iota(square, 0), iota(square, 1)
    cluster_col = jnp.sum(jnp.where(i0 == i1, cluster_row, 0), axis=1, keepdims=True)
    slot_row = jnp.sum(
        jnp.where((cluster_col == cluster_row) & (i0 < i1), 1, 0), axis=0, keepdims=True)
    flat_row = (cluster_row // 2) * side + (cluster_row % 2) * bucket + slot_row
    place[...] = jnp.where(iota(place.shape, 0) == flat_row, 1.0, 0.0).astype(BF16)

    rank = priority_ref[...]
    high, low = (rank // 128).astype(F32), (rank % 128).astype(F32)
    line = iota((8, rows), 0)
    meta = jnp.where(line == 0, high, jnp.where(line == 1, low, jnp.where(line == 2, 1.0, 0.0)))
    meta = meta.astype(BF16)

    def rank_block(to, _):
        s = iota((128, rows), 0)
        hit = (s + to * per_owner == flat_row) & (s < per_owner)
        got = lax.dot_general(
            meta, jnp.where(hit, 1.0, 0.0).astype(BF16), (((1,), (1,)), ((), ())),
            preferred_element_type=F32)
        line = got[0:1] * 128.0 + got[1:2] + (1.0 - got[2:3]) * float(sentinel)
        send_r[to] = jnp.broadcast_to(line, (8, 128))
        return 0

    lax.fori_loop(0, owners, rank_block, 0)
    recv_r[me] = send_r[me]

    def project(i):
        span = pl.ds(i * half, half)
        xs = x_v[span, :]
        wide = xs.astype(F32)
        scaling = lax.rsqrt(jnp.sum(wide * wide, axis=1, keepdims=True) * (1.0 / width) + 1e-05)
        gained = xs * gain_ref[...].reshape(1, width)
        product = jnp.dot(gained, vw_v[...], preferred_element_type=F32)
        values[span, :] = (product * scaling).astype(BF16)

    load_x(0).wait()
    load_vw.wait()
    project(0)
    load_x(1).wait()
    project(1)
    load_ow.wait()
    pl.semaphore_wait(barrier, 3 + owners - 1)

    def copy_a(k):
        return pltpu.make_async_remote_copy(
            send_a.at[k], recv_a.at[k], a_s.at[k], a_r.at[k], device_id=(me, partner), device_id_type=MESH)

    def copy_b(k):
        return pltpu.make_async_remote_copy(
            send_b.at[k], recv_b.at[k], b_s.at[k], b_r.at[k], device_id=(me, across), device_id_type=MESH)

    def start_c(k, h):
        each_peer(lambda to: pltpu.make_async_remote_copy(
            send_c.at[k, to, h], recv_c.at[k, h, me], c_s.at[k, h], c_r.at[k, h],
            device_id=(to, t), device_id_type=MESH).start())
        recv_c[k, h, me] = send_c[k, me, h]

    def term(quarter, k):
        columns = pl.ds(pl.multiple_of(quarter * part + k * chunk, chunk), chunk)
        w = ow_v[:, columns].astype(F32)
        kv_local = values.shape[1] // HEAD_DIM
        w = w.reshape(kv_local, HEADS // KV_HEADS, HEAD_DIM, chunk)
        w = jnp.sum(w, axis=1).reshape(kv_local * HEAD_DIM, chunk).astype(BF16)
        return jnp.dot(values[...], w, preferred_element_type=F32).astype(BF16)

    def stage_a(k):
        for h in range(2):
            send_a[k, h] = term(2 * h + 1 - core, k)
        copy_a(k).start()
        for h in range(2):
            keep_a[k, h] = term(2 * h + core, k)

    def stage_b(k):
        copy_a(k).wait_recv()
        send_b[k] = (keep_a[k, 1 - xh].astype(F32) + recv_a[k, 1 - xh].astype(F32)).astype(BF16)
        copy_b(k).start()

    def stage_c(k):
        copy_b(k).wait_recv()
        columns = pl.ds(pl.multiple_of(t * part + k * chunk, chunk), chunk)
        attention = keep_a[k, xh].astype(F32) + recv_a[k, xh].astype(F32) + recv_b[k].astype(F32)
        hidden = (x_v[:, columns].astype(F32) + attention).astype(BF16)
        placed = jnp.dot(place[...], hidden, preferred_element_type=F32).astype(BF16)
        send_c[k] = placed.reshape(owners, 2, side, chunk)
        start_c(k, 1 - xh)

        @pl.when(k % 2 == 1)
        def _():
            start_c(k // 2, xh)

    def step(s, _):
        @pl.when(s < chunks)
        def _():
            stage_a(s)

        @pl.when((s > 0) & (s <= chunks))
        def _():
            stage_b(s - 1)

        @pl.when(s >= LAG)
        def _():
            stage_c(s - LAG)

        return 0

    lax.fori_loop(0, chunks + LAG, step, 0)
    lax.fori_loop(chunks // 2, chunks, lambda k, _: start_c(k, xh) or 0, 0)
    each_peer(lambda to: pltpu.make_async_remote_copy(
        send_r.at[to], recv_r.at[me], r_s, r_r, device_id=(to, t), device_id_type=MESH).start())

    others = pl.ds(0, owners - 1)
    gram[...] = jnp.zeros_like(gram)

    def stage_d(h):
        def one(k, _):
            drain(recv_c.at[k, h, others], c_r.at[k, h])
            for c in range(2):
                if bucket % 16 == 0:
                    members = recv_c[k, h, :, c * bucket:(c + 1) * bucket, :].reshape(capacity, chunk)
                else:
                    every = recv_c[k, h].reshape(owners * side, chunk)
                    shape = (capacity, owners * side)
                    r = iota(shape, 0)
                    pick = (r // bucket) * side + c * bucket + r % bucket == iota(shape, 1)
                    members = jnp.dot(
                        jnp.where(pick, 1.0, 0.0).astype(BF16), every, preferred_element_type=F32)
                    members = members.astype(BF16)
                gram[2 * h + c] += lax.dot_general(
                    members, members, (((1,), (1,)), ((), ())), preferred_element_type=F32)
            return 0

        lax.fori_loop(0, chunks, one, 0)

    def copy_e(h):
        return pltpu.make_async_remote_copy(
            gram.at[2 * h + 1 - core], recv_e.at[h], e_s.at[h], e_r.at[h],
            device_id=(me, partner), device_id_type=MESH)

    copy_f = pltpu.make_async_remote_copy(
        send_f, recv_f, f_s, f_r, device_id=(me, across), device_id_type=MESH)

    stage_d(1 - xh)
    copy_e(1 - xh).start()
    copy_e(1 - xh).wait_recv()
    send_f[...] = gram[2 * (1 - xh) + core] + recv_e[1 - xh]
    copy_f.start()

    drain(recv_r.at[others], r_r)
    ranks = recv_r[:, 0, :]
    r = iota((capacity, owners), 0)
    expand = jnp.where(r // bucket == iota((capacity, owners), 1), 1.0, 0.0)
    spread = jnp.dot(expand, ranks, precision=lax.Precision.HIGHEST, preferred_element_type=F32)
    r = iota((capacity, 128), 0)
    lane = xh * side + core * bucket + r % bucket
    rank_col = jnp.sum(
        jnp.where(iota((capacity, 128), 1) == lane, spread, 0.0), axis=1, keepdims=True)
    eye = iota((capacity, capacity), 0) == iota((capacity, capacity), 1)
    rank_row = jnp.sum(jnp.where(eye, rank_col, 0.0), axis=0, keepdims=True)
    pick = jnp.where(iota((capacity, rows), 0) == me * bucket + slot_row, 1.0, 0.0)

    stage_d(xh)
    copy_e(xh).start()
    copy_f.wait_recv()
    copy_e(xh).wait_recv()
    total = gram[2 * xh + core] + recv_e[xh] + recv_f[...]
    diagonal = jnp.where(eye, total, 0.0)
    norm_row = lax.rsqrt(jnp.sum(diagonal, axis=0, keepdims=True) + 1e-06)
    norm_col = lax.rsqrt(jnp.sum(diagonal, axis=1, keepdims=True) + 1e-06)
    similarity = total * norm_col * norm_row
    highest = jnp.max(jnp.where(rank_col < rank_row, similarity, -2.0), axis=0, keepdims=True)
    highest = jnp.maximum(highest, -1.0)
    best_t[t] = jnp.broadcast_to(highest, (8, capacity))

    def copy_g(to, frm):
        return pltpu.make_async_remote_copy(
            best_t.at[frm], best_t.at[frm], g_s.at[to], g_r.at[frm], device_id=(me, to), device_id_type=MESH)

    for o in range(1, 4):
        copy_g(lax.rem(t + o, 4), t).start()
    for o in range(1, 4):
        copy_g(t, lax.rem(t + o, 4)).wait_recv()
    line = iota((8, capacity), 0)
    rows_h = jnp.zeros((8, capacity), F32)
    for c in range(CLU_DEV):
        rows_h = jnp.where(line == c, best_t[c], rows_h)
    send_h[...] = rows_h
    each_peer(lambda to: pltpu.make_async_remote_copy(
        send_h, recv_h.at[me], h_s, h_r, device_id=(to, t), device_id_type=MESH).start())
    recv_h[me] = rows_h
    drain(recv_h.at[others], h_r)
    returned = recv_h[...].reshape(owners * 8, capacity)
    found = jnp.dot(returned, pick, precision=lax.Precision.HIGHEST, preferred_element_type=F32)
    where = (cluster_row // CLU_DEV) * 8 + cluster_row % CLU_DEV
    out_ref[...] = jnp.sum(
        jnp.where(iota((owners * 8, rows), 0) == where, found, 0.0), axis=0, keepdims=True)

    def sent_k(k, _):
        copy_a(k).wait_send()
        copy_b(k).wait_send()
        for h in range(2):
            drain(recv_c.at[k, h, others], c_s.at[k, h])
        return 0

    lax.fori_loop(0, chunks, sent_k, 0)
    drain(recv_r.at[others], r_s)
    drain(recv_h.at[others], h_s)
    copy_e(1 - xh).wait_send()
    copy_e(xh).wait_send()
    copy_f.wait_send()
    for o in range(1, 4):
        copy_g(lax.rem(t + o, 4), t).wait_send()


def shards(final_input, norm_gain, value_weight, out_weight, cluster, priority):
    rows, width = final_input.shape
    owners = lax.axis_size("dp")
    tensor = lax.axis_size("tensor")
    part = width // tensor
    chunk = part // CHUNKS
    bucket = max(2, 2 * rows // (CLU_DEV * owners))
    side = max(16, 2 * bucket)
    per_owner = 2 * side
    capacity = owners * bucket
    kv = value_weight.shape[1]
    vmem = pl.BlockSpec(memory_space=pltpu.VMEM)
    anywhere = pl.BlockSpec(memory_space=pl.ANY)
    dma = pltpu.SemaphoreType.DMA
    best = pl.pallas_call(
        functools.partial(kernel, owners, bucket),
        out_shape=jax.ShapeDtypeStruct((1, rows), F32),
        in_specs=[anywhere, vmem, anywhere, anywhere, vmem, vmem],
        out_specs=vmem,
        scratch_shapes=[
            pltpu.VMEM((rows, width), BF16),
            pltpu.VMEM((width, kv), BF16),
            pltpu.VMEM(out_weight.shape, BF16),
            pltpu.VMEM((rows, kv), BF16),
            pltpu.VMEM((CHUNKS, 2, rows, chunk), BF16),
            pltpu.VMEM((CHUNKS, 2, rows, chunk), BF16),
            pltpu.VMEM((CHUNKS, 2, rows, chunk), BF16),
            pltpu.VMEM((CHUNKS, rows, chunk), BF16),
            pltpu.VMEM((CHUNKS, rows, chunk), BF16),
            pltpu.VMEM((owners * per_owner, rows), BF16),
            pltpu.VMEM((CHUNKS, owners, 2, side, chunk), BF16),
            pltpu.VMEM((CHUNKS, 2, owners, side, chunk), BF16),
            pltpu.VMEM((owners, 8, 128), F32),
            pltpu.VMEM((owners, 8, 128), F32),
            pltpu.VMEM((CLU_DEV, capacity, capacity), F32),
            pltpu.VMEM((2, capacity, capacity), F32),
            pltpu.VMEM((capacity, capacity), F32),
            pltpu.VMEM((capacity, capacity), F32),
            pltpu.VMEM((CLU_DEV, 8, capacity), F32),
            pltpu.VMEM((8, capacity), F32),
            pltpu.VMEM((owners, 8, capacity), F32),
            dma((4,)),
            dma((CHUNKS,)), dma((CHUNKS,)),
            dma((CHUNKS,)), dma((CHUNKS,)),
            dma((CHUNKS, 2)), dma((CHUNKS, 2)),
            dma, dma,
            dma((2,)), dma((2,)),
            dma, dma,
            dma((4,)), dma((4,)),
            dma, dma,
        ],
        compiler_params=pltpu.CompilerParams(
            collective_id=0, has_side_effects=True, vmem_limit_bytes=56 * 1024 * 1024),
        cost_estimate=pl.CostEstimate(flops=6_000_000_000, bytes_accessed=16_000_000, transcendentals=0),
    )(final_input, norm_gain, value_weight, out_weight, cluster.reshape(1, rows), priority.reshape(1, rows))
    return best.reshape(rows)


def solution(mesh):
    in_specs = (P("dp", None), P(), P(None, "tensor"), P("tensor", None), P("dp", None), P("dp"))
    out_specs = P("dp")
    return jax.shard_map(shards, mesh=mesh, in_specs=in_specs, out_specs=out_specs, check_vma=False)
```

time: 89.6 us -> 76.6 us (0.85)
  Pallas kernels: 85.2 us -> 75.1 us
  local copies, waits for them, and re-layouts: 4.08 us -> 1.26 us
    pallas_call x1, Pallas kernels: 85.2 us -> 75.1 us  [shards(): pl.pallas_call(functools.partial(kernel, owners, bucket), out_shape=jax.S...]
    unnamed x2 -> x1, local copies, waits for them, and re-layouts: 2.77 us -> 1.26 us
    reshape x1 -> x0, local copies, waits for them, and re-layouts: 1.3 us -> none  [shards(): norm_gain.reshape(1, width)]
where the time goes in v2:
time: 76.6 us; the launch traced here: 76.4 us
  Pallas kernels  75.1 us (98%)
  local copies, waits for them, and re-layouts  1.26 us (2%)
    pallas_call x1, Pallas kernels, shards(): pl.pallas_call(functools.partial(kernel, owners, bucket), out_shape=jax.S...  75.1 us

profile of v2, /device:TPU:0, one launch (start us, length us, event | category | flops | bytes accessed | tf_op | source)
XLA Modules:
  0.0 76.4 jit_solution(4541851120411526861)
XLA Ops:
  0.0 75.1 %shard_map.64 = f32[1,512]{1,0:T(1,128)} custom-call(bf16[512,4096]{1,0:T(8,128)(2,1)} %x_hbm.1, bf16[4096]{0:T(1024)(128)(2,1)} %gain_ref.1, bf16[4096,256]{1,0:T(8,128)(2,1)} %vw_hbm.1, bf16[1024,4096]{1,0:T(8,128)(2,1)} %ow_hbm.1, s32[1,512]{1,0:T(1,128)} %bitcast.4, s32[1,512]{1,0:T(1,128)} %bitcast.5), custom_call_target="tpu_custom_call" | custom-call | flops 6000000000 | bytes 16000000 | tf_op jit(solution)/shard_map/pallas_call | solution.py:310
  75.1 1.3 %copy.8 = f32[512]{0:T(512)} copy(f32[512]{0:T(512)} %bitcast.3) | data formatting | bytes 4096

commit v3 on v2

--- a/solution.py
+++ b/solution.py
@@ -30,7 +30,7 @@
 def kernel(
     owners, bucket,
     x_hbm, gain_ref, vw_hbm, ow_hbm, cluster_ref, priority_ref, out_ref,
-    x_v, vw_v, ow_v, values, send_a, keep_a, recv_a, send_b, recv_b,
+    x_v, vw_v, ow_v, scale_v, values, send_a, keep_a, recv_a, send_b, recv_b,
     place, send_c, recv_c, send_r, recv_r, gram, recv_e, send_f, recv_f, best_t, send_h, recv_h,
     in_sem, a_s, a_r, b_s, b_r, c_s, c_r, r_s, r_r, e_s, e_r, f_s, f_r, g_s, g_r, h_s, h_r,
 ):
@@ -71,7 +71,6 @@
     load_x(0).start()
     load_vw.start()
     load_x(1).start()
-    load_ow.start()
 
     barrier = pltpu.get_barrier_semaphore()
     for o in range(1, 4):
@@ -87,6 +86,94 @@
     flat_row = (cluster_row // 2) * side + (cluster_row % 2) * bucket + slot_row
     place[...] = jnp.where(iota(place.shape, 0) == flat_row, 1.0, 0.0).astype(BF16)
 
+    def project(i):
+        span = pl.ds(i * half, half)
+        xs = x_v[span, :]
+        gained = xs * gain_ref[...].reshape(1, width)
+        values[span, :] = jnp.dot(gained, vw_v[...], preferred_element_type=F32).astype(BF16)
+
+    load_x(0).wait()
+    load_vw.wait()
+    load_ow.start()
+    project(0)
+    load_x(1).wait()
+    project(1)
+    load_ow.wait()
+    pl.semaphore_wait(barrier, 3 + owners - 1)
+
+    def copy_a(k):
+        return pltpu.make_async_remote_copy(
+            send_a.at[k], recv_a.at[k], a_s.at[k], a_r.at[k], device_id=(me, partner), device_id_type=MESH)
+
+    def copy_b(k):
+        return pltpu.make_async_remote_copy(
+            send_b.at[k], recv_b.at[k], b_s.at[k], b_r.at[k], device_id=(me, across), device_id_type=MESH)
+
+    def start_c(k, h):
+        each_peer(lambda to: pltpu.make_async_remote_copy(
+            send_c.at[k, to, h], recv_c.at[k, h, me], c_s.at[k, h], c_r.at[k, h],
+            device_id=(to, t), device_id_type=MESH).start())
+        recv_c[k, h, me] = send_c[k, me, h]
+
+    def term(quarter, k):
+        columns = pl.ds(pl.multiple_of(quarter * part + k * chunk, chunk), chunk)
+        w = ow_v[:, columns].astype(F32)
+        kv_local = values.shape[1] // HEAD_DIM
+        w = w.reshape(kv_local, HEADS // KV_HEADS, HEAD_DIM, chunk)
+        w = jnp.sum(w, axis=1).reshape(kv_local * HEAD_DIM, chunk).astype(BF16)
+        return jnp.dot(values[...], w, preferred_element_type=F32).astype(BF16)
+
+    def stage_a(k):
+        for h in range(2):
+            send_a[k, h] = term(2 * h + 1 - core, k)
+        copy_a(k).start()
+        for h in range(2):
+            keep_a[k, h] = term(2 * h + core, k)
+
+    def stage_b(k):
+        copy_a(k).wait_recv()
+        send_b[k] = (keep_a[k, 1 - xh].astype(F32) + recv_a[k, 1 - xh].astype(F32)).astype(BF16)
+        copy_b(k).start()
+
+    def stage_c(k):
+        copy_b(k).wait_recv()
+        columns = pl.ds(pl.multiple_of(t * part + k * chunk, chunk), chunk)
+        attention = keep_a[k, xh].astype(F32) + recv_a[k, xh].astype(F32) + recv_b[k].astype(F32)
+        hidden = (x_v[:, columns].astype(F32) + attention * scale_v[...]).astype(BF16)
+        placed = jnp.dot(place[...], hidden, preferred_element_type=F32).astype(BF16)
+        send_c[k] = placed.reshape(owners, 2, side, chunk)
+        start_c(k, 1 - xh)
+
+        @pl.when(k % 2 == 1)
+        def _():
+            start_c(k // 2, xh)
+
+    def step(s, _):
+        @pl.when(s < chunks)
+        def _():
+            stage_a(s)
+
+        @pl.when((s > 0) & (s <= chunks))
+        def _():
+            stage_b(s - 1)
+
+        @pl.when(s >= LAG)
+        def _():
+            stage_c(s - LAG)
+
+        return 0
+
+    lax.fori_loop(0, 2, step, 0)
+
+    def row_scale(i, _):
+        span = pl.ds(pl.multiple_of(i * 128, 128), 128)
+        xs = x_v[span, :].astype(F32)
+        scale_v[span, :] = lax.rsqrt(jnp.sum(xs * xs, axis=1, keepdims=True) * (1.0 / width) + 1e-05)
+        return 0
+
+    lax.fori_loop(0, rows // 128, row_scale, 0)
+    lax.fori_loop(2, chunks + LAG, step, 0)
+    lax.fori_loop(chunks // 2, chunks, lambda k, _: start_c(k, xh) or 0, 0)
     rank = priority_ref[...]
     high, low = (rank // 128).astype(F32), (rank % 128).astype(F32)
     line = iota((8, rows), 0)
@@ -105,88 +192,6 @@
 
     lax.fori_loop(0, owners, rank_block, 0)
     recv_r[me] = send_r[me]
-
-    def project(i):
-        span = pl.ds(i * half, half)
-        xs = x_v[span, :]
-        wide = xs.astype(F32)
-        scaling = lax.rsqrt(jnp.sum(wide * wide, axis=1, keepdims=True) * (1.0 / width) + 1e-05)
-        gained = xs * gain_ref[...].reshape(1, width)
-        product = jnp.dot(gained, vw_v[...], preferred_element_type=F32)
-        values[span, :] = (product * scaling).astype(BF16)
-
-    load_x(0).wait()
-    load_vw.wait()
-    project(0)
-    load_x(1).wait()
-    project(1)
-    load_ow.wait()
-    pl.semaphore_wait(barrier, 3 + owners - 1)
-
-    def copy_a(k):
-        return pltpu.make_async_remote_copy(
-            send_a.at[k], recv_a.at[k], a_s.at[k], a_r.at[k], device_id=(me, partner), device_id_type=MESH)
-
-    def copy_b(k):
-        return pltpu.make_async_remote_copy(
-            send_b.at[k], recv_b.at[k], b_s.at[k], b_r.at[k], device_id=(me, across), device_id_type=MESH)
-
-    def start_c(k, h):
-        each_peer(lambda to: pltpu.make_async_remote_copy(
-            send_c.at[k, to, h], recv_c.at[k, h, me], c_s.at[k, h], c_r.at[k, h],
-            device_id=(to, t), device_id_type=MESH).start())
-        recv_c[k, h, me] = send_c[k, me, h]
-
-    def term(quarter, k):
-        columns = pl.ds(pl.multiple_of(quarter * part + k * chunk, chunk), chunk)
-        w = ow_v[:, columns].astype(F32)
-        kv_local = values.shape[1] // HEAD_DIM
-        w = w.reshape(kv_local, HEADS // KV_HEADS, HEAD_DIM, chunk)
-        w = jnp.sum(w, axis=1).reshape(kv_local * HEAD_DIM, chunk).astype(BF16)
-        return jnp.dot(values[...], w, preferred_element_type=F32).astype(BF16)
-
-    def stage_a(k):
-        for h in range(2):
-            send_a[k, h] = term(2 * h + 1 - core, k)
-        copy_a(k).start()
-        for h in range(2):
-            keep_a[k, h] = term(2 * h + core, k)
-
-    def stage_b(k):
-        copy_a(k).wait_recv()
-        send_b[k] = (keep_a[k, 1 - xh].astype(F32) + recv_a[k, 1 - xh].astype(F32)).astype(BF16)
-        copy_b(k).start()
-
-    def stage_c(k):
-        copy_b(k).wait_recv()
-        columns = pl.ds(pl.multiple_of(t * part + k * chunk, chunk), chunk)
-        attention = keep_a[k, xh].astype(F32) + recv_a[k, xh].astype(F32) + recv_b[k].astype(F32)
-        hidden = (x_v[:, columns].astype(F32) + attention).astype(BF16)
-        placed = jnp.dot(place[...], hidden, preferred_element_type=F32).astype(BF16)
-        send_c[k] = placed.reshape(owners, 2, side, chunk)
-        start_c(k, 1 - xh)
-
-        @pl.when(k % 2 == 1)
-        def _():
-            start_c(k // 2, xh)
-
-    def step(s, _):
-        @pl.when(s < chunks)
-        def _():
-            stage_a(s)
-
-        @pl.when((s > 0) & (s <= chunks))
-        def _():
-            stage_b(s - 1)
-
-        @pl.when(s >= LAG)
-        def _():
-            stage_c(s - LAG)
-
-        return 0
-
-    lax.fori_loop(0, chunks + LAG, step, 0)
-    lax.fori_loop(chunks // 2, chunks, lambda k, _: start_c(k, xh) or 0, 0)
     each_peer(lambda to: pltpu.make_async_remote_copy(
         send_r.at[to], recv_r.at[me], r_s, r_r, device_id=(to, t), device_id_type=MESH).start())
 
@@ -238,7 +243,8 @@
         jnp.where(iota((capacity, 128), 1) == lane, spread, 0.0), axis=1, keepdims=True)
     eye = iota((capacity, capacity), 0) == iota((capacity, capacity), 1)
     rank_row = jnp.sum(jnp.where(eye, rank_col, 0.0), axis=0, keepdims=True)
-    pick = jnp.where(iota((capacity, rows), 0) == me * bucket + slot_row, 1.0, 0.0)
+    spot = me * bucket + slot_row
+    pick = jnp.where(iota((128, rows), 0) == spot % 128, 1.0, 0.0)
 
     stage_d(xh)
     copy_e(xh).start()
@@ -261,18 +267,19 @@
         copy_g(lax.rem(t + o, 4), t).start()
     for o in range(1, 4):
         copy_g(t, lax.rem(t + o, 4)).wait_recv()
-    line = iota((8, capacity), 0)
-    rows_h = jnp.zeros((8, capacity), F32)
+    line = iota((8, 128), 0)
+    rows_h = jnp.zeros((8, 128), F32)
     for c in range(CLU_DEV):
-        rows_h = jnp.where(line == c, best_t[c], rows_h)
+        for j in range(2):
+            rows_h = jnp.where(line == j * CLU_DEV + c, best_t[c, :, j * 128:(j + 1) * 128], rows_h)
     send_h[...] = rows_h
     each_peer(lambda to: pltpu.make_async_remote_copy(
         send_h, recv_h.at[me], h_s, h_r, device_id=(to, t), device_id_type=MESH).start())
     recv_h[me] = rows_h
     drain(recv_h.at[others], h_r)
-    returned = recv_h[...].reshape(owners * 8, capacity)
+    returned = recv_h[...].reshape(owners * 8, 128)
     found = jnp.dot(returned, pick, precision=lax.Precision.HIGHEST, preferred_element_type=F32)
-    where = (cluster_row // CLU_DEV) * 8 + cluster_row % CLU_DEV
+    where = (cluster_row // CLU_DEV) * 8 + (spot // 128) * CLU_DEV + cluster_row % CLU_DEV
     out_ref[...] = jnp.sum(
         jnp.where(iota((owners * 8, rows), 0) == where, found, 0.0), axis=0, keepdims=True)
 
@@ -316,6 +323,7 @@
             pltpu.VMEM((rows, width), BF16),
             pltpu.VMEM((width, kv), BF16),
             pltpu.VMEM(out_weight.shape, BF16),
+            pltpu.VMEM((rows, 1), F32),
             pltpu.VMEM((rows, kv), BF16),
             pltpu.VMEM((CHUNKS, 2, rows, chunk), BF16),
             pltpu.VMEM((CHUNKS, 2, rows, chunk), BF16),
@@ -332,8 +340,8 @@
             pltpu.VMEM((capacity, capacity), F32),
             pltpu.VMEM((capacity, capacity), F32),
             pltpu.VMEM((CLU_DEV, 8, capacity), F32),
-            pltpu.VMEM((8, capacity), F32),
-            pltpu.VMEM((owners, 8, capacity), F32),
+            pltpu.VMEM((8, 128), F32),
+            pltpu.VMEM((owners, 8, 128), F32),
             dma((4,)),
             dma((CHUNKS,)), dma((CHUNKS,)),
             dma((CHUNKS,)), dma((CHUNKS,)),

time: 76.6 us -> 77.7 us (1.014)
  Pallas kernels: 75.1 us -> 76.2 us
    pallas_call x1, Pallas kernels: 75.1 us -> 76.2 us  [shards(): pl.pallas_call(functools.partial(kernel, owners, bucket), out_shape=jax.S...]
where the time goes in v3:
time: 77.7 us; the launch traced here: 77.5 us
  Pallas kernels  76.2 us (98%)
  local copies, waits for them, and re-layouts  1.26 us (2%)
    pallas_call x1, Pallas kernels, shards(): pl.pallas_call(functools.partial(kernel, owners, bucket), out_shape=jax.S...  76.2 us

profile of v3, /device:TPU:0, one launch (start us, length us, event | category | flops | bytes accessed | tf_op | source)
XLA Modules:
  0.0 77.5 jit_solution(12835935777141051572)
XLA Ops:
  0.0 76.2 %shard_map.64 = f32[1,512]{1,0:T(1,128)} custom-call(bf16[512,4096]{1,0:T(8,128)(2,1)} %x_hbm.1, bf16[4096]{0:T(1024)(128)(2,1)} %gain_ref.1, bf16[4096,256]{1,0:T(8,128)(2,1)} %vw_hbm.1, bf16[1024,4096]{1,0:T(8,128)(2,1)} %ow_hbm.1, s32[1,512]{1,0:T(1,128)} %bitcast.4, s32[1,512]{1,0:T(1,128)} %bitcast.5), custom_call_target="tpu_custom_call" | custom-call | flops 6000000000 | bytes 16000000 | tf_op jit(solution)/shard_map/pallas_call | solution.py:317
  76.2 1.3 %copy.8 = f32[512]{0:T(512)} copy(f32[512]{0:T(512)} %bitcast.3) | data formatting | bytes 4096

commit v4 on v3

--- a/solution.py
+++ b/solution.py
@@ -11,8 +11,8 @@
 KV_HEADS = 8
 HEAD_DIM = 128
 CLU_DEV = 4
-CHUNKS = 8
-LAG = 5
+CHUNKS = 4
+LAG = 3
 MESH = pl.DeviceIdType.MESH
 BF16 = jnp.bfloat16
 F32 = jnp.float32
@@ -172,8 +172,6 @@
         return 0
 
     lax.fori_loop(0, rows // 128, row_scale, 0)
-    lax.fori_loop(2, chunks + LAG, step, 0)
-    lax.fori_loop(chunks // 2, chunks, lambda k, _: start_c(k, xh) or 0, 0)
     rank = priority_ref[...]
     high, low = (rank // 128).astype(F32), (rank % 128).astype(F32)
     line = iota((8, rows), 0)
@@ -195,6 +193,8 @@
     each_peer(lambda to: pltpu.make_async_remote_copy(
         send_r.at[to], recv_r.at[me], r_s, r_r, device_id=(to, t), device_id_type=MESH).start())
 
+    lax.fori_loop(2, chunks + LAG, step, 0)
+    lax.fori_loop(chunks // 2, chunks, lambda k, _: start_c(k, xh) or 0, 0)
     others = pl.ds(0, owners - 1)
     gram[...] = jnp.zeros_like(gram)
 

time: 77.7 us -> 77.7 us (level)
  no operation moved by 1% of the time
where the time goes in v4:
time: 77.7 us; the launch traced here: 77.5 us
  Pallas kernels  76.2 us (98%)
  local copies, waits for them, and re-layouts  1.26 us (2%)
    pallas_call x1, Pallas kernels, shards(): pl.pallas_call(functools.partial(kernel, owners, bucket), out_shape=jax.S...  76.2 us

profile of v4, /device:TPU:0, one launch (start us, length us, event | category | flops | bytes accessed | tf_op | source)
XLA Modules:
  0.0 77.5 jit_solution(5990861703310977771)
XLA Ops:
  0.0 76.2 %shard_map.64 = f32[1,512]{1,0:T(1,128)} custom-call(bf16[512,4096]{1,0:T(8,128)(2,1)} %x_hbm.1, bf16[4096]{0:T(1024)(128)(2,1)} %gain_ref.1, bf16[4096,256]{1,0:T(8,128)(2,1)} %vw_hbm.1, bf16[1024,4096]{1,0:T(8,128)(2,1)} %ow_hbm.1, s32[1,512]{1,0:T(1,128)} %bitcast.4, s32[1,512]{1,0:T(1,128)} %bitcast.5), custom_call_target="tpu_custom_call" | custom-call | flops 6000000000 | bytes 16000000 | tf_op jit(solution)/shard_map/pallas_call | solution.py:317
  76.2 1.3 %copy.8 = f32[512]{0:T(512)} copy(f32[512]{0:T(512)} %bitcast.3) | data formatting | bytes 4096

commit v5 on v4

--- a/solution.py
+++ b/solution.py
@@ -11,8 +11,8 @@
 KV_HEADS = 8
 HEAD_DIM = 128
 CLU_DEV = 4
-CHUNKS = 4
-LAG = 3
+CHUNKS = 8
+LAG = 5
 MESH = pl.DeviceIdType.MESH
 BF16 = jnp.bfloat16
 F32 = jnp.float32
@@ -67,10 +67,16 @@
         return pltpu.make_async_copy(x_hbm.at[span], x_v.at[span], in_sem.at[i])
 
     load_vw = pltpu.make_async_copy(vw_hbm, vw_v, in_sem.at[2])
-    load_ow = pltpu.make_async_copy(ow_hbm, ow_v, in_sem.at[3])
+
+    def load_ow(start, size, sem):
+        for q in range(4):
+            span = pl.ds(q * part + start, size)
+            pltpu.make_async_copy(ow_hbm.at[:, span], ow_v.at[:, span], sem).start()
+
     load_x(0).start()
     load_vw.start()
     load_x(1).start()
+    load_ow(0, chunk, in_sem.at[3])
 
     barrier = pltpu.get_barrier_semaphore()
     for o in range(1, 4):
@@ -94,11 +100,11 @@
 
     load_x(0).wait()
     load_vw.wait()
-    load_ow.start()
+    load_ow(chunk, part - chunk, in_sem.at[4])
     project(0)
     load_x(1).wait()
     project(1)
-    load_ow.wait()
+    drain(ow_v.at[:, pl.ds(0, 4 * chunk)], in_sem.at[3])
     pl.semaphore_wait(barrier, 3 + owners - 1)
 
     def copy_a(k):
@@ -144,11 +150,15 @@
         send_c[k] = placed.reshape(owners, 2, side, chunk)
         start_c(k, 1 - xh)
 
-        @pl.when(k % 2 == 1)
+        @pl.when(k % 2 == 0)
         def _():
             start_c(k // 2, xh)
 
     def step(s, _):
+        @pl.when(s == 1)
+        def _():
+            drain(ow_v.at[:, pl.ds(0, 4 * (part - chunk))], in_sem.at[4])
+
         @pl.when(s < chunks)
         def _():
             stage_a(s)
@@ -342,7 +352,7 @@
             pltpu.VMEM((CLU_DEV, 8, capacity), F32),
             pltpu.VMEM((8, 128), F32),
             pltpu.VMEM((owners, 8, 128), F32),
-            dma((4,)),
+            dma((5,)),
             dma((CHUNKS,)), dma((CHUNKS,)),
             dma((CHUNKS,)), dma((CHUNKS,)),
             dma((CHUNKS, 2)), dma((CHUNKS, 2)),

time: 77.7 us -> 77.2 us (level)
  no operation moved by 1% of the time
where the time goes in v5:
time: 77.2 us; the launch traced here: 77 us
  Pallas kernels  75.7 us (98%)
  local copies, waits for them, and re-layouts  1.26 us (2%)
    pallas_call x1, Pallas kernels, shards(): pl.pallas_call(functools.partial(kernel, owners, bucket), out_shape=jax.S...  75.7 us

profile of v5, /device:TPU:0, one launch (start us, length us, event | category | flops | bytes accessed | tf_op | source)
XLA Modules:
  0.0 77.0 jit_solution(18118760956637544854)
XLA Ops:
  0.0 75.7 %shard_map.64 = f32[1,512]{1,0:T(1,128)} custom-call(bf16[512,4096]{1,0:T(8,128)(2,1)} %x_hbm.1, bf16[4096]{0:T(1024)(128)(2,1)} %gain_ref.1, bf16[4096,256]{1,0:T(8,128)(2,1)} %vw_hbm.1, bf16[1024,4096]{1,0:T(8,128)(2,1)} %ow_hbm.1, s32[1,512]{1,0:T(1,128)} %bitcast.4, s32[1,512]{1,0:T(1,128)} %bitcast.5), custom_call_target="tpu_custom_call" | custom-call | flops 6000000000 | bytes 16000000 | tf_op jit(solution)/shard_map/pallas_call | solution.py:327
  75.7 1.3 %copy.8 = f32[512]{0:T(512)} copy(f32[512]{0:T(512)} %bitcast.3) | data formatting | bytes 4096

commit v6 on v5

--- a/solution.py
+++ b/solution.py
@@ -12,7 +12,8 @@
 HEAD_DIM = 128
 CLU_DEV = 4
 CHUNKS = 8
-LAG = 5
+LAG = 2
+HELD = 2
 MESH = pl.DeviceIdType.MESH
 BF16 = jnp.bfloat16
 F32 = jnp.float32
@@ -204,7 +205,7 @@
         send_r.at[to], recv_r.at[me], r_s, r_r, device_id=(to, t), device_id_type=MESH).start())
 
     lax.fori_loop(2, chunks + LAG, step, 0)
-    lax.fori_loop(chunks // 2, chunks, lambda k, _: start_c(k, xh) or 0, 0)
+    lax.fori_loop(chunks // 2, chunks - HELD, lambda k, _: start_c(k, xh) or 0, 0)
     others = pl.ds(0, owners - 1)
     gram[...] = jnp.zeros_like(gram)
 
@@ -241,6 +242,7 @@
     copy_e(1 - xh).wait_recv()
     send_f[...] = gram[2 * (1 - xh) + core] + recv_e[1 - xh]
     copy_f.start()
+    lax.fori_loop(chunks - HELD, chunks, lambda k, _: start_c(k, xh) or 0, 0)
 
     drain(recv_r.at[others], r_r)
     ranks = recv_r[:, 0, :]

time: 77.2 us -> 73.9 us (0.957)
  Pallas kernels: 75.7 us -> 72.5 us
    pallas_call x1, Pallas kernels: 75.7 us -> 72.5 us  [shards(): pl.pallas_call(functools.partial(kernel, owners, bucket), out_shape=jax.S...]
where the time goes in v6:
time: 73.9 us; the launch traced here: 73.7 us
  Pallas kernels  72.5 us (98%)
  local copies, waits for them, and re-layouts  1.26 us (2%)
    pallas_call x1, Pallas kernels, shards(): pl.pallas_call(functools.partial(kernel, owners, bucket), out_shape=jax.S...  72.5 us

profile of v6, /device:TPU:0, one launch (start us, length us, event | category | flops | bytes accessed | tf_op | source)
XLA Modules:
  0.0 73.7 jit_solution(4759412823268212901)
XLA Ops:
  0.0 72.5 %shard_map.64 = f32[1,512]{1,0:T(1,128)} custom-call(bf16[512,4096]{1,0:T(8,128)(2,1)} %x_hbm.1, bf16[4096]{0:T(1024)(128)(2,1)} %gain_ref.1, bf16[4096,256]{1,0:T(8,128)(2,1)} %vw_hbm.1, bf16[1024,4096]{1,0:T(8,128)(2,1)} %ow_hbm.1, s32[1,512]{1,0:T(1,128)} %bitcast.4, s32[1,512]{1,0:T(1,128)} %bitcast.5), custom_call_target="tpu_custom_call" | custom-call | flops 6000000000 | bytes 16000000 | tf_op jit(solution)/shard_map/pallas_call | solution.py:329
  72.5 1.3 %copy.8 = f32[512]{0:T(512)} copy(f32[512]{0:T(512)} %bitcast.3) | data formatting | bytes 4096

commit v7 on v6

--- a/solution.py
+++ b/solution.py
@@ -56,9 +56,11 @@
             bit = 2 * bit
         return found
 
+    turn = 2 * (2 * ((me // 2) % 2) + core)
+
     def each_peer(act):
         def step(i, _):
-            act(peer(owners - 1 - i))
+            act(peer(lax.rem(i + turn, owners - 1) + 1))
             return 0
 
         lax.fori_loop(0, owners - 1, step, 0)

time: 73.9 us -> 75.4 us (1.020)
  Pallas kernels: 72.5 us -> 73.9 us
    pallas_call x1, Pallas kernels: 72.5 us -> 73.9 us  [shards(): pl.pallas_call(functools.partial(kernel, owners, bucket), out_shape=jax.S...]
where the time goes in v7:
time: 75.4 us; the launch traced here: 75.2 us
  Pallas kernels  73.9 us (98%)
  local copies, waits for them, and re-layouts  1.26 us (2%)
    pallas_call x1, Pallas kernels, shards(): pl.pallas_call(functools.partial(kernel, owners, bucket), out_shape=jax.S...  73.9 us

profile of v7, /device:TPU:0, one launch (start us, length us, event | category | flops | bytes accessed | tf_op | source)
XLA Modules:
  0.0 75.2 jit_solution(17741188646468300691)
XLA Ops:
  0.0 73.9 %shard_map.64 = f32[1,512]{1,0:T(1,128)} custom-call(bf16[512,4096]{1,0:T(8,128)(2,1)} %x_hbm.1, bf16[4096]{0:T(1024)(128)(2,1)} %gain_ref.1, bf16[4096,256]{1,0:T(8,128)(2,1)} %vw_hbm.1, bf16[1024,4096]{1,0:T(8,128)(2,1)} %ow_hbm.1, s32[1,512]{1,0:T(1,128)} %bitcast.4, s32[1,512]{1,0:T(1,128)} %bitcast.5), custom_call_target="tpu_custom_call" | custom-call | flops 6000000000 | bytes 16000000 | tf_op jit(solution)/shard_map/pallas_call | solution.py:331
  73.9 1.3 %copy.8 = f32[512]{0:T(512)} copy(f32[512]{0:T(512)} %bitcast.3) | data formatting | bytes 4096

commit v8 on v6

--- a/solution.py
+++ b/solution.py
@@ -58,7 +58,7 @@
 
     def each_peer(act):
         def step(i, _):
-            act(peer(owners - 1 - i))
+            act(peer(owners - 1 - i // 2 - lax.rem(i, 2) * (owners // 2)))
             return 0
 
         lax.fori_loop(0, owners - 1, step, 0)

time: 73.9 us -> 73.6 us (level)
  no operation moved by 1% of the time
where the time goes in v8:
time: 73.6 us; the launch traced here: 73.4 us
  Pallas kernels  72.1 us (98%)
  local copies, waits for them, and re-layouts  1.26 us (2%)
    pallas_call x1, Pallas kernels, shards(): pl.pallas_call(functools.partial(kernel, owners, bucket), out_shape=jax.S...  72.1 us

profile of v8, /device:TPU:0, one launch (start us, length us, event | category | flops | bytes accessed | tf_op | source)
XLA Modules:
  0.0 73.4 jit_solution(10737088523799914875)
XLA Ops:
  0.0 72.1 %shard_map.64 = f32[1,512]{1,0:T(1,128)} custom-call(bf16[512,4096]{1,0:T(8,128)(2,1)} %x_hbm.1, bf16[4096]{0:T(1024)(128)(2,1)} %gain_ref.1, bf16[4096,256]{1,0:T(8,128)(2,1)} %vw_hbm.1, bf16[1024,4096]{1,0:T(8,128)(2,1)} %ow_hbm.1, s32[1,512]{1,0:T(1,128)} %bitcast.4, s32[1,512]{1,0:T(1,128)} %bitcast.5), custom_call_target="tpu_custom_call" | custom-call | flops 6000000000 | bytes 16000000 | tf_op jit(solution)/shard_map/pallas_call | solution.py:329
  72.1 1.3 %copy.8 = f32[512]{0:T(512)} copy(f32[512]{0:T(512)} %bitcast.3) | data formatting | bytes 4096

commit v9 on v8

--- a/solution.py
+++ b/solution.py
@@ -13,7 +13,7 @@
 CLU_DEV = 4
 CHUNKS = 8
 LAG = 2
-HELD = 2
+HELD = 3
 MESH = pl.DeviceIdType.MESH
 BF16 = jnp.bfloat16
 F32 = jnp.float32

time: 73.6 us -> 75.6 us (1.027)
  Pallas kernels: 72.1 us -> 74.1 us
    pallas_call x1, Pallas kernels: 72.1 us -> 74.1 us  [shards(): pl.pallas_call(functools.partial(kernel, owners, bucket), out_shape=jax.S...]
where the time goes in v9:
time: 75.6 us; the launch traced here: 75.3 us
  Pallas kernels  74.1 us (98%)
  local copies, waits for them, and re-layouts  1.26 us (2%)
    pallas_call x1, Pallas kernels, shards(): pl.pallas_call(functools.partial(kernel, owners, bucket), out_shape=jax.S...  74.1 us

profile of v9, /device:TPU:0, one launch (start us, length us, event | category | flops | bytes accessed | tf_op | source)
XLA Modules:
  0.0 75.3 jit_solution(9217918452671899052)
XLA Ops:
  0.0 74.1 %shard_map.64 = f32[1,512]{1,0:T(1,128)} custom-call(bf16[512,4096]{1,0:T(8,128)(2,1)} %x_hbm.1, bf16[4096]{0:T(1024)(128)(2,1)} %gain_ref.1, bf16[4096,256]{1,0:T(8,128)(2,1)} %vw_hbm.1, bf16[1024,4096]{1,0:T(8,128)(2,1)} %ow_hbm.1, s32[1,512]{1,0:T(1,128)} %bitcast.4, s32[1,512]{1,0:T(1,128)} %bitcast.5), custom_call_target="tpu_custom_call" | custom-call | flops 6000000000 | bytes 16000000 | tf_op jit(solution)/shard_map/pallas_call | solution.py:329
  74.1 1.3 %copy.8 = f32[512]{0:T(512)} copy(f32[512]{0:T(512)} %bitcast.3) | data formatting | bytes 4096
